TPU v7x, 32 devices: a whole 2x2x4 slice. The times are simulated.
32 devices in a mesh: expert: 4 (over x, core), context: 2 (over y), dp: 4 (over z).
Axes of the slice: x: 2, y: 2, z: 4, core: 2. Of those that a mesh axis runs over, the one named last changes fastest.
Arguments:
- tokens: bfloat16 [16, 512, 1024], P(('expert', 'dp'), 'context'), may hold values from -6 to 6
- span_order: int32 [4], replicated, may hold values from 0 to 3, each once
- routes: int32 [16, 512, 8], P(('expert', 'dp'), 'context'), may hold values from 0 to 15, all different within a row; in each aligned block of 256 rows (0 to 255, 256 to 511, ..., all dimensions but the last counted through in order) at most 160 rows name the same one
- norm_attn: bfloat16 [1024], replicated, may hold values from 0.5 to 1.5
- w_query: bfloat16 [1024, 1024], replicated, may hold values from -0.1875 to 0.1875
- w_key: bfloat16 [1024, 512], replicated, may hold values from -0.1875 to 0.1875
- w_value: bfloat16 [1024, 512], replicated, may hold values from -0.1875 to 0.1875
- w_out: bfloat16 [1024, 1024], replicated, may hold values from -1.5 to 1.5
- norm_moe: bfloat16 [1024], replicated, may hold values from 0.5 to 1.5
- w_router: bfloat16 [1024, 16], replicated, may hold values from -0.09375 to 0.09375
- w_gate: bfloat16 [16, 1024, 512], P('expert'), may hold values from -0.1875 to 0.1875
- w_up: bfloat16 [16, 1024, 512], P('expert'), may hold values from -0.1875 to 0.1875
- w_down: bfloat16 [16, 512, 1024], P('expert'), may hold values from -1 to 1
- cotangent: bfloat16 [16, 512, 1024], P(('expert', 'dp'), 'context'), may hold values from -6 to 6
Outputs:
- outputs: bfloat16 [16, 512, 1024], P(('expert', 'dp'), 'context')
- grad_tokens: bfloat16 [16, 512, 1024], P(('expert', 'dp'), 'context')
- grad_norm_attn: float32 [1024], replicated
- grad_query: float32 [1024, 1024], replicated
- grad_key: float32 [1024, 512], replicated
- grad_value: float32 [1024, 512], replicated
- grad_out: float32 [1024, 1024], replicated
- grad_norm_moe: float32 [1024], replicated
- grad_router: float32 [1024, 16], replicated
- grad_gate: float32 [16, 1024, 512], P('expert')
- grad_up: float32 [16, 1024, 512], P('expert')
- grad_down: float32 [16, 512, 1024], P('expert')
Inputs may be any that keep to these rules, and one draw needn't show every extreme that they name: span_order is a permutation; stored block j of every sequence holds the tokens at positions span_order[j] * 128 to span_order[j] * 128 + 127. `routes`: each token names 8 different experts. Within the rows of one device (aligned blocks of 256 rows, in order), no expert is named by more than 160 rows, a bound that some block reaches.
All inputs are finite; a program needn't handle non-finite values.
Results may differ from a plain program's by a relative error of at most 0.017.
Values may be sent and summed in bfloat16 or wider, within the bound.
A program may use at most 192 MiB of HBM per device.

v0:
```python
import math
import jax
import jax.numpy as jnp
from jax import lax
from jax.sharding import PartitionSpec as P

H = 16
KV = 8
HD = 64
EXPERTS = 16
SPAN = 128
EPSILON = 1e-06
ROPE_BASE = 10000.0
MASKED = -1e30
F32 = jnp.float32
BF16 = jnp.bfloat16


def rope_tables(positions):
    half_dim = HD // 2
    frequency = ROPE_BASE ** (-(jnp.arange(half_dim, dtype=F32) * 2.0) / HD)
    angles = positions.astype(F32)[:, None] * frequency[None, :]
    return (jnp.cos(angles), jnp.sin(angles))


def rotate(tensor, cos_table, sin_table):
    half_dim = tensor.shape[-1] // 2
    front = tensor[..., :half_dim]
    back = tensor[..., half_dim:]
    cos_wide = cos_table[:, None, :]
    sin_wide = sin_table[:, None, :]
    return jnp.concatenate(
        [front * cos_wide - back * sin_wide, back * cos_wide + front * sin_wide], axis=-1
    )


def positions_of(row_index, span_order):
    block_ids = row_index // SPAN
    picked = jnp.where(
        block_ids[:, None] == jnp.arange(span_order.shape[0], dtype=jnp.int32)[None, :],
        span_order[None, :],
        0,
    )
    return jnp.sum(picked, axis=1, dtype=jnp.int32) * SPAN + row_index % SPAN


def norm_back(grad_normed, normed, inv_root):
    return inv_root * (
        grad_normed - normed * jnp.mean(grad_normed * normed, axis=-1, keepdims=True)
    )


def dot(a, b):
    return jnp.dot(a, b, preferred_element_type=F32)


def dot_t(a, b):
    return lax.dot_general(a, b, (((1,), (1,)), ((), ())), preferred_element_type=F32)


def t_dot(a, b):
    return lax.dot_general(a, b, (((0,), (0,)), ((), ())), preferred_element_type=F32)


def body(
    tokens,
    span_order,
    routes,
    norm_attn,
    w_query,
    w_key,
    w_value,
    w_out,
    norm_moe,
    w_router,
    w_gate,
    w_up,
    w_down,
    cotangent,
):
    tok_rows = tokens.shape[1]
    width = tokens.shape[2]
    seq_rows = tok_rows * lax.axis_size("context")
    groups = H // KV
    score_scale = 1.0 / math.sqrt(HD)
    local_experts = w_gate.shape[0]
    ff = w_gate.shape[2]
    dy_all = lax.all_gather(cotangent[0], "expert", axis=0, tiled=True)
    routes_all = lax.all_gather(routes[0], "expert", axis=0, tiled=True)
    local_index = lax.axis_index("context") * tok_rows + jnp.arange(tok_rows, dtype=jnp.int32)
    pos_query = positions_of(local_index, span_order)
    pos_keys = positions_of(jnp.arange(seq_rows, dtype=jnp.int32), span_order)
    cos_table, sin_table = rope_tables(pos_query)
    allowed = pos_keys[None, :] <= pos_query[:, None]
    inputs = tokens[0].astype(F32)
    inv_one = lax.rsqrt(jnp.mean(inputs * inputs, axis=-1, keepdims=True) + EPSILON)
    normed_one = inputs * inv_one
    gain_one = norm_attn.astype(F32)
    h_one = (normed_one * gain_one).astype(BF16)
    key_pre = dot(h_one, w_key).reshape(tok_rows, KV, HD)
    keys_local = rotate(key_pre, cos_table, sin_table).astype(BF16).reshape(tok_rows, KV * HD)
    values_local = dot(h_one, w_value).astype(BF16)
    kv_all = lax.all_gather(
        jnp.concatenate([keys_local, values_local], axis=1), "context", axis=0, tiled=True
    )
    query_pre = dot(h_one, w_query).reshape(tok_rows, H, HD)
    queries = rotate(query_pre, cos_table, sin_table).astype(BF16).reshape(tok_rows, KV, groups, HD)
    keys_all = kv_all[:, : KV * HD].reshape(seq_rows, KV, HD)
    values_all = kv_all[:, KV * HD :].reshape(seq_rows, KV, HD)
    scores = (
        jnp.einsum("qkgd,skd->kgqs", queries, keys_all, preferred_element_type=F32) * score_scale
    )
    masked = jnp.where(allowed, scores, MASKED)
    top_score = jnp.max(masked, axis=-1, keepdims=True)
    exp_scores = jnp.exp(masked - top_score)
    total_exp = jnp.sum(exp_scores, axis=-1, keepdims=True)
    attn_probs = exp_scores / total_exp
    probs_rounded = attn_probs.astype(BF16)
    mixed_heads = jnp.einsum(
        "kgqs,skd->qkgd", probs_rounded, values_all, preferred_element_type=F32
    )
    mixed_heads = mixed_heads.reshape(tok_rows, H * HD).astype(BF16)
    y_one = inputs + dot(mixed_heads, w_out)
    inv_two = lax.rsqrt(jnp.mean(y_one * y_one, axis=-1, keepdims=True) + EPSILON)
    normed_two = y_one * inv_two
    gain_two = norm_moe.astype(F32)
    h_two = (normed_two * gain_two).astype(BF16)
    h_all = lax.all_gather(h_two, "expert", axis=0, tiled=True)
    experts = jnp.arange(EXPERTS, dtype=jnp.int32)
    chosen = jnp.any(routes_all[:, :, None] == experts[None, None, :], axis=1)
    logits = jnp.where(chosen, dot(h_all, w_router), MASKED)
    weights = jnp.where(chosen, jnp.exp(logits - jnp.max(logits, axis=-1, keepdims=True)), 0.0)
    weights = weights / jnp.sum(weights, axis=-1, keepdims=True)
    me = lax.axis_index("expert")
    mine = lax.dynamic_slice_in_dim(weights, me * local_experts, local_experts, axis=1)
    partial_y = None
    partial_h = None
    dots = []
    g_gate, g_up, g_down = ([], [], [])
    for e in range(local_experts):
        weight = mine[:, e : e + 1]
        gate_pre = dot(h_all, w_gate[e])
        upward = dot(h_all, w_up[e])
        back = dot_t(dy_all, w_down[e])
        sigmoid_gate = jax.nn.sigmoid(gate_pre)
        silu_gate = gate_pre * sigmoid_gate
        hidden = silu_gate * upward
        hidden_w = (hidden * weight).astype(BF16)
        dots.append(jnp.sum(hidden * back, axis=-1, keepdims=True))
        grad_hidden = back * weight
        grad_gate_pre = (
            grad_hidden * upward * sigmoid_gate * (1.0 + gate_pre * (1.0 - sigmoid_gate))
        ).astype(BF16)
        grad_up_pre = (grad_hidden * silu_gate).astype(BF16)
        add_y = dot(hidden_w, w_down[e])
        add_h = dot_t(grad_gate_pre, w_gate[e]) + dot_t(grad_up_pre, w_up[e])
        partial_y = add_y if partial_y is None else partial_y + add_y
        partial_h = add_h if partial_h is None else partial_h + add_h
        g_down.append(t_dot(hidden_w, dy_all).astype(BF16))
        g_gate.append(t_dot(h_all, grad_gate_pre).astype(BF16))
        g_up.append(t_dot(h_all, grad_up_pre).astype(BF16))
    d_weights = jnp.concatenate(dots, axis=1)
    d_wide = lax.dynamic_update_slice_in_dim(
        jnp.zeros((d_weights.shape[0], EXPERTS), F32), d_weights, me * local_experts, axis=1
    )
    d_high = lax.reduce_precision(d_wide, 8, 7)
    packed = jnp.concatenate(
        [
            partial_h.astype(BF16),
            d_high.astype(BF16),
            (d_wide - d_high).astype(BF16),
            jnp.zeros((d_wide.shape[0], 128 - 2 * EXPERTS), BF16),
        ],
        axis=1,
    )
    home = lax.psum_scatter(packed, "expert", scatter_dimension=0, tiled=True).astype(F32)
    y_two = lax.psum_scatter(
        partial_y.astype(BF16), "expert", scatter_dimension=0, tiled=True
    ).astype(F32)
    total_gate, total_up, total_down = (
        lax.psum(jnp.stack(g), ("context", "dp")).astype(F32) for g in (g_gate, g_up, g_down)
    )
    outputs = (y_one + y_two).astype(BF16)[None]
    grad_final = cotangent[0].astype(F32)
    grad_weights = home[:, width : width + EXPERTS] + home[:, width + EXPERTS : width + 2 * EXPERTS]
    own = lax.dynamic_slice_in_dim(weights, me * tok_rows, tok_rows, axis=0)
    grad_logits = (
        own * (grad_weights - jnp.sum(own * grad_weights, axis=-1, keepdims=True))
    ).astype(BF16)
    grad_router_w = t_dot(h_two, grad_logits)
    grad_h_two = home[:, :width] + dot_t(grad_logits, w_router)
    grad_gain_two = jnp.sum(grad_h_two * normed_two, axis=0)
    grad_y_one = grad_final + norm_back(grad_h_two * gain_two, normed_two, inv_two)
    grad_attn = grad_y_one.astype(BF16)
    grad_out_w = t_dot(mixed_heads, grad_attn)
    grad_mixed = dot_t(grad_attn, w_out).astype(BF16).reshape(tok_rows, KV, groups, HD)
    grad_probs = jnp.einsum("qkgd,skd->kgqs", grad_mixed, values_all, preferred_element_type=F32)
    grad_values = jnp.einsum(
        "kgqs,qkgd->skd", probs_rounded, grad_mixed, preferred_element_type=F32
    )
    row_dots = jnp.sum(attn_probs * grad_probs, axis=-1, keepdims=True)
    grad_scores = (attn_probs * (grad_probs - row_dots)).astype(BF16)
    grad_keys = (
        jnp.einsum("kgqs,qkgd->skd", grad_scores, queries, preferred_element_type=F32) * score_scale
    )
    grad_kv = lax.psum_scatter(
        jnp.concatenate(
            [grad_keys.reshape(seq_rows, KV * HD), grad_values.reshape(seq_rows, KV * HD)], axis=1
        ).astype(BF16),
        "context",
        scatter_dimension=0,
        tiled=True,
    ).astype(F32)
    grad_queries = (
        jnp.einsum("kgqs,skd->qkgd", grad_scores, keys_all, preferred_element_type=F32)
        * score_scale
    )
    grad_q_pre = (
        rotate(grad_queries.reshape(tok_rows, H, HD), cos_table, -sin_table)
        .reshape(tok_rows, H * HD)
        .astype(BF16)
    )
    grad_k_pre = (
        rotate(grad_kv[:, : KV * HD].reshape(tok_rows, KV, HD), cos_table, -sin_table)
        .reshape(tok_rows, KV * HD)
        .astype(BF16)
    )
    grad_v_pre = grad_kv[:, KV * HD :].astype(BF16)
    grad_query_w = t_dot(h_one, grad_q_pre)
    grad_key_w = t_dot(h_one, grad_k_pre)
    grad_value_w = t_dot(h_one, grad_v_pre)
    grad_h_one = dot_t(grad_q_pre, w_query) + dot_t(grad_k_pre, w_key) + dot_t(grad_v_pre, w_value)
    grad_gain_one = jnp.sum(grad_h_one * normed_one, axis=0)
    grad_inputs = grad_y_one + norm_back(grad_h_one * gain_one, normed_one, inv_one)
    grad_tokens = grad_inputs.astype(BF16)[None]
    everywhere = ("expert", "context", "dp")
    total_o = lax.psum(grad_out_w.astype(BF16), everywhere).astype(F32)
    total_q, total_k, total_v = (
        t.astype(F32)
        for t in lax.psum(
            tuple((g.astype(BF16) for g in (grad_query_w, grad_key_w, grad_value_w))), everywhere
        )
    )
    total_g1, total_g2, total_r = lax.psum(
        (grad_gain_one, grad_gain_two, grad_router_w), everywhere
    )
    return (
        outputs,
        grad_tokens,
        total_g1,
        total_q,
        total_k,
        total_v,
        total_o,
        total_g2,
        total_r,
        total_gate,
        total_up,
        total_down,
    )


def solution(mesh):
    in_specs = (
        P(("expert", "dp"), "context", None),
        P(),
        P(("expert", "dp"), "context", None),
        P(),
        P(),
        P(),
        P(),
        P(),
        P(),
        P(),
        P("expert", None, None),
        P("expert", None, None),
        P("expert", None, None),
        P(("expert", "dp"), "context", None),
    )
    out_specs = (
        P(("expert", "dp"), "context", None),
        P(("expert", "dp"), "context", None),
        P(),
        P(),
        P(),
        P(),
        P(),
        P(),
        P(),
        P("expert", None, None),
        P("expert", None, None),
        P("expert", None, None),
    )
    return jax.shard_map(body, mesh=mesh, in_specs=in_specs, out_specs=out_specs, check_vma=False)
```

profile of v0, /device:TPU:1, one launch (start us, length us, event | category | flops | bytes accessed | tf_op | source)
XLA Modules:
  0.0 959.9 jit_solution(15199929937461508150)
XLA Ops:
  19.1 3.9 copy.122
  27.2 14.6 %all-gather.6.cloned.1.call-done = bf16[512,1024]{1,0:T(8,128)(2,1)} async-done(((bf16[256,1024]{1,0:T(8,128)(2,1)}), bf16[512,1024]{1,0:T(8,128)(2,1)}) %all-gather.6.cloned.1.call-update) | async-done | bytes 1048592 | tf_op jit(solution)/shard_map/all_gather | solution.py:103
  46.1 8.0 fusion.203
  54.1 4.3 fusion.74
  61.6 6.1 all-gather
  67.9 4.6 fusion.16
  80.3 11.1 %all-gather.8.cloned.1.call-done = bf16[1024,1024]{0,1:T(8,128)(2,1)} async-done(((bf16[256,1024]{0,1:T(8,128)(2,1)}), bf16[1024,1024]{0,1:T(8,128)(2,1)}) %all-gather.8.cloned.1.call-update) | async-done | bytes 2097168 | tf_op jit(solution)/shard_map/all_gather | solution.py:128
  134.0 9.2 add_convert_fusion
  156.7 4.3 fusion.47
  167.9 11.0 %reduce-scatter.6.cloned.1.call-done = bf16[256,1152]{0,1:T(8,128)(2,1)} async-done(((bf16[1024,1152]{0,1:T(8,128)(2,1)}), bf16[256,1152]{0,1:T(8,128)(2,1)}) %reduce-scatter.6.cloned.1.call-update) | async-done | bytes 589840 | tf_op jit(solution)/shard_map/reduce_scatter | solution.py:176
  182.5 30.9 %reduce-scatter.4.cloned.1.call-done = bf16[256,1024]{0,1:T(8,128)(2,1)} async-done(((bf16[1024,1024]{0,1:T(8,128)(2,1)}), bf16[256,1024]{0,1:T(8,128)(2,1)}) %reduce-scatter.4.cloned.1.call-update) | async-done | bytes 524304 | tf_op jit(solution)/shard_map/reduce_scatter | solution.py:177
  218.9 4.9 fusion.1
  223.8 4.8 fusion.78
  228.6 4.5 fusion.3
  236.8 4.0 fusion.51
  249.7 7.0 reduce-scatter.8.cloned.1.call-done
  291.6 39.5 %all-reduce = (f32[1024]{0:T(1024)}, f32[1024]{0:T(1024)}) all-reduce(f32[1024]{0:T(1024)S(1)} %get-tuple-element.26, f32[1024]{0:T(1024)S(1)} %get-tuple-element.24), channel_id=1, replica_groups=mesh['expert'=4,'context'=2,'dp'=4] {'expert','context','dp'}, use_global_device_ids=true, to_apply=%region_21.22 | all-reduce | flops 2048 | bytes 16384 | tf_op jit(solution)/shard_map/psum | solution.py:244
  331.1 90.1 %all-reduce.9.cloned.1.call-done = (bf16[1024,1024]{1,0:T(8,128)(2,1)}, bf16[1024,512]{1,0:T(8,128)(2,1)}, bf16[1024,512]{1,0:T(8,128)(2,1)}, bf16[1024,1024]{1,0:T(8,128)(2,1)}) async-done(((bf16[1024,1024]{1,0:T(8,128)(2,1)}, bf16[1024,512]{1,0:T(8,128)(2,1)}, bf16[1024,512]{1,0:T(8,128)(2,1)}, bf16[1024,1024]{1,0:T(8,128)(2,1)}), (bf16[1024,1024]{1,0:T(8,128)(2,1)}, bf16[1024,512]{1,0:T(8,128)(2,1)}, ...) | async-done | bytes 6291472 | tf_op jit(solution)/shard_map/psum | solution.py:240
  421.2 4.2 convert_element_type.280
  431.8 394.5 %all-reduce.11.cloned.1.call-done = (bf16[4,1024,512]{2,1,0:T(8,128)(2,1)}, bf16[4,1024,512]{2,1,0:T(8,128)(2,1)}, bf16[4,512,1024]{2,1,0:T(8,128)(2,1)}) async-done(((bf16[4,1024,512]{2,1,0:T(8,128)(2,1)}, bf16[4,1024,512]{2,1,0:T(8,128)(2,1)}, bf16[4,512,1024]{2,1,0:T(8,128)(2,1)}), (bf16[4,1024,512]{2,1,0:T(8,128)(2,1)}, bf16[4,1024,512]{2,1,0:T(8,128)(2,1)}, ...) | async-done | bytes 12582928 | tf_op jit(solution)/shard_map/psum | solution.py:181
  826.2 6.9 convert_element_type.291
  833.1 4.6 convert_element_type.296
  837.7 4.4 convert_element_type.301
  842.2 109.5 %all-reduce.7.cloned.1.call-done = f32[1024,16]{0,1:T(8,128)} async-done(((f32[1024,16]{0,1:T(8,128)}), f32[1024,16]{0,1:T(8,128)}) %all-reduce.7.cloned.1.call-update) | async-done | bytes 65552 | tf_op jit(solution)/shard_map/psum | solution.py:244
  (304 shorter events, 157.8 us)
Async XLA Ops:
  7.2 51.3 %copy-start = (bf16[1024,1024]{1,0:T(8,128)(2,1)S(1)}, bf16[1024,1024]{1,0:T(8,128)(2,1)}, u32[]{:S(2)}) copy-start(bf16[1024,1024]{1,0:T(8,128)(2,1)} %param.21) | copy-start | bytes 6291460
  7.2 34.6 %all-gather.6.cloned.1.call-start = ((), (), s32[]{:S(2)}) async-start(), calls=%async_computation.3 | async-start | bytes 1572864 | tf_op jit(solution)/shard_map/all_gather | solution.py:103
  8.6 49.8 %copy-start.3 = (bf16[1,256,1024]{1,2,0:T(8,128)(2,1)}, bf16[1,256,1024]{1,2,0:T(8,128)(2,1)S(1)}, u32[]{:S(2)}) copy-start(bf16[1,256,1024]{1,2,0:T(8,128)(2,1)S(1)} %copy.116) | copy-start | bytes 1572868
  9.4 13.6 %copy-start.62 = (f32[1024]{0:T(1024)}, f32[1024]{0:T(1024)S(1)}, u32[]{:S(2)}) copy-start(f32[1024]{0:T(1024)S(1)} %convert_element_type.237) | copy-start | bytes 12292
  9.5 13.5 %copy-start.64 = (f32[256]{0:T(256)}, f32[256]{0:T(256)S(1)}, u32[]{:S(2)}) copy-start(f32[256]{0:T(256)S(1)} %add_rsqrt_fusion.1) | copy-start | bytes 3076
  18.2 49.6 %all-gather.10.cloned.1.call-start = ((), (), s32[]{:S(2)}) async-start(), calls=%async_computation.9 | async-start | bytes 2621440 | tf_op jit(solution)/shard_map/all_gather | solution.py:88
  18.9 72.4 %all-gather.8.cloned.1.call-start = ((), (), s32[]{:S(2)}) async-start(), calls=%async_computation.4 | async-start | bytes 2621440 | tf_op jit(solution)/shard_map/all_gather | solution.py:128
  27.2 18.9 %copy-start.43 = (bf16[256,16,32]{0,2,1:T(8,128)(2,1)}, bf16[256,16,32]{0,2,1:T(8,128)(2,1)S(1)}, u32[]{:S(2)}) copy-start(bf16[256,16,32]{0,2,1:T(8,128)(2,1)S(1)} %get-tuple-element.57) | copy-start | bytes 786436
  27.2 18.9 %copy-start.61 = (pred[256,512]{0,1:T(8,128)(4,1)S(1)}, pred[256,512]{0,1:T(8,128)(4,1)}, u32[]{:S(2)}) copy-start(pred[256,512]{0,1:T(8,128)(4,1)} %broadcast_compare_fusion) | copy-start | bytes 393220
  61.5 117.4 %reduce-scatter.6.cloned.1.call-start = ((), (), s32[]{:S(2)}) async-start(), calls=%async_computation.6 | async-start | bytes 2949120 | tf_op jit(solution)/shard_map/reduce_scatter | solution.py:176
  77.7 13.7 %copy-start.59 = (bf16[1024,16]{0,1:T(8,128)(2,1)S(1)}, bf16[1024,16]{0,1:T(8,128)(2,1)}, u32[]{:S(2)}) copy-start(bf16[1024,16]{0,1:T(8,128)(2,1)} %param.23) | copy-start | bytes 98308
  106.3 10.5 %copy-start.78 = (bf16[1024,512]{0,1:T(8,128)(2,1)}, bf16[1024,512]{0,1:T(8,128)(2,1)S(1)}, u32[]{:S(2)}) copy-start(bf16[1024,512]{0,1:T(8,128)(2,1)S(1)} %get-tuple-element.45) | copy-start | bytes 3145732
  109.0 37.1 %copy-start.24 = (bf16[1024,512]{0,1:T(8,128)(2,1)}, bf16[1024,512]{0,1:T(8,128)(2,1)S(1)}, u32[]{:S(2)}) copy-start(bf16[1024,512]{0,1:T(8,128)(2,1)S(1)} %get-tuple-element.54) | copy-start | bytes 3145732
  112.5 11.4 %copy-start.73 = (bf16[1024,512]{0,1:T(8,128)(2,1)}, bf16[1024,512]{0,1:T(8,128)(2,1)S(1)}, u32[]{:S(2)}) copy-start(bf16[1024,512]{0,1:T(8,128)(2,1)S(1)} %get-tuple-element.51) | copy-start | bytes 3145732
  116.0 11.2 %copy-start.83 = (bf16[1024,512]{0,1:T(8,128)(2,1)}, bf16[1024,512]{0,1:T(8,128)(2,1)S(1)}, u32[]{:S(2)}) copy-start(bf16[1024,512]{0,1:T(8,128)(2,1)S(1)} %get-tuple-element.39) | copy-start | bytes 3145732
  116.0 14.7 %copy-start.74 = (bf16[1024,512]{0,1:T(8,128)(2,1)}, bf16[1024,512]{0,1:T(8,128)(2,1)S(1)}, u32[]{:S(2)}) copy-start(bf16[1024,512]{0,1:T(8,128)(2,1)S(1)} %get-tuple-element.49) | copy-start | bytes 3145732
  146.0 67.4 %reduce-scatter.4.cloned.1.call-start = ((), (), s32[]{:S(2)}) async-start(), calls=%async_computation.5 | async-start | bytes 2621440 | tf_op jit(solution)/shard_map/reduce_scatter | solution.py:177
  154.7 102.0 %reduce-scatter.8.cloned.1.call-start = ((), (), s32[]{:S(2)}) async-start(), calls=%async_computation.7 | async-start | bytes 1572864 | tf_op jit(solution)/shard_map/reduce_scatter | solution.py:206
  165.6 14.4 %copy-start.58 = (f32[1024,16]{0,1:T(8,128)S(1)}, f32[1024,16]{0,1:T(8,128)}, u32[]{:S(2)}) copy-start(f32[1024,16]{0,1:T(8,128)} %copy-done.57) | copy-start | bytes 196612
  165.6 15.4 %copy-start.9 = (f32[256,1024]{0,1:T(8,128)S(1)}, f32[256,1024]{0,1:T(8,128)}, u32[]{:S(2)}) copy-start(f32[256,1024]{0,1:T(8,128)} %copy-done.8) | copy-start | bytes 3145732
  165.6 15.4 %copy-start.60 = (bf16[1024,16]{0,1:T(8,128)(2,1)S(1)}, bf16[1024,16]{0,1:T(8,128)(2,1)}, u32[]{:S(2)}) copy-start(bf16[1024,16]{0,1:T(8,128)(2,1)} %param.23) | copy-start | bytes 98308
  236.3 184.9 %all-reduce.9.cloned.1.call-start = ((), (), s32[]{:S(2)}) async-start(), calls=%async_computation.10 | async-start | bytes 12582912 | tf_op jit(solution)/shard_map/psum | solution.py:240
  260.9 565.3 %all-reduce.11.cloned.1.call-start = ((), (), s32[]{:S(2)}) async-start(), calls=%async_computation.11 | async-start | bytes 25165824 | tf_op jit(solution)/shard_map/psum | solution.py:181
  279.6 672.0 %all-reduce.7.cloned.1.call-start = ((), (), s32[]{:S(2)}) async-start(), calls=%async_computation.8 | async-start | bytes 131072 | tf_op jit(solution)/shard_map/psum | solution.py:244
  (74 other events, 223.1 us)
Sparse Core Ops, SparseCore 0:
  18.3 23.4 all-gather.5
  43.3 22.9 all-gather.9
  68.5 22.8 all-gather.7
  146.2 32.6 reduce-scatter.5
  181.9 31.4 reduce-scatter.3
  236.4 20.3 reduce-scatter.7
  264.4 156.7 all-reduce.8
  426.4 399.7 all-reduce.10
  833.3 118.3 all-reduce.6
where the time goes:
time: 967 us; the launch traced here: 960 us
  waiting for transfers between devices  669 us (69%)
  matrix products  145 us (15%)
  other arithmetic  52.2 us (5%)
  blocking collectives  45.6 us (5%)
  local copies, waits for them, and re-layouts  31.9 us (3%)
  between operations  15.1 us (2%)
    psum x1, waiting for transfers between devices, body(): lax.psum(jnp.stack(g), ('context', 'dp')).astype(F32)  394 us
    psum x1, waiting for transfers between devices, body(): lax.psum((grad_gain_one, grad_gain_two, grad_router_w), everywhere)  110 us
    psum x1, waiting for transfers between devices, body(): lax.psum(tuple((g.astype(BF16) for g in (grad_query_w, grad_key_w, grad_v...  90.1 us
    dot_general x17, matrix products, dot_t(): lax.dot_general(a, b, (((1,), (1,)), ((), ())), preferred_element_type=F32)  47.2 us
    psum x1, blocking collectives, body(): lax.psum((grad_gain_one, grad_gain_two, grad_router_w), everywhere)  39.5 us
    dot_general x17, matrix products, dot(): return jnp.dot(a, b, preferred_element_type=F32)  37.3 us
    dot_general x17, matrix products, t_dot(): lax.dot_general(a, b, (((0,), (0,)), ((), ())), preferred_element_type=F32)  35.9 us
    reduce_scatter x1, waiting for transfers between devices, body(): lax.psum_scatter(partial_y.astype(BF16), 'expert', scatter_dimension=0, t...  30.9 us
  transfers between devices with their start and end apart: 9, of which 8 were waited for; matrix products, arithmetic and copies ran while one was open for 13% of the time, Pallas kernels for 0%

commit v1 on v0

--- a/solution.py
+++ b/solution.py
@@ -178,7 +178,8 @@
         partial_y.astype(BF16), "expert", scatter_dimension=0, tiled=True
     ).astype(F32)
     total_gate, total_up, total_down = (
-        lax.psum(jnp.stack(g), ("context", "dp")).astype(F32) for g in (g_gate, g_up, g_down)
+        lax.psum(lax.psum(jnp.stack(g), "dp"), "context").astype(F32)
+        for g in (g_gate, g_up, g_down)
     )
     outputs = (y_one + y_two).astype(BF16)[None]
     grad_final = cotangent[0].astype(F32)

time: 967 us -> 1290 us (1.33)
  waiting for transfers between devices: 669 us -> 984 us
    psum x1 -> x2, waiting for transfers between devices: 394 us -> 706 us  [the longest x1 424 us: body(): lax.psum(jnp.stack(g), 'dp')]
    psum x1, waiting for transfers between devices: 90.1 us -> 112 us  [body(): lax.psum(tuple((g.astype(BF16) for g in (grad_query_w, grad_key_w, grad_v...]
    unnamed x185 -> x189, local copies, waits for them, and re-layouts: 25.4 us -> 25.9 us
  transfers between devices with their start and end apart: 9 -> 10, of which waited for: 8 -> 7; matrix products, arithmetic and copies ran while one was open for 13% -> 10% of each run, Pallas kernels for 0% -> 0%
where the time goes in v1:
time: 1290 us; the launch traced here: 1280 us
  waiting for transfers between devices  984 us (76%)
  matrix products  147 us (11%)
  other arithmetic  52.2 us (4%)
  blocking collectives  46 us (4%)
  local copies, waits for them, and re-layouts  32.4 us (3%)
  between operations  15.4 us (1%)
    psum x1, waiting for transfers between devices, body(): lax.psum(jnp.stack(g), 'dp')  424 us
    psum x1, waiting for transfers between devices, body(): lax.psum(lax.psum(jnp.stack(g), 'dp'), 'context').astype(F32)  282 us
    psum x1, waiting for transfers between devices, body(): lax.psum(tuple((g.astype(BF16) for g in (grad_query_w, grad_key_w, grad_v...  112 us
    psum x1, waiting for transfers between devices, body(): lax.psum((grad_gain_one, grad_gain_two, grad_router_w), everywhere)  109 us
    dot_general x17, matrix products, dot_t(): lax.dot_general(a, b, (((1,), (1,)), ((), ())), preferred_element_type=F32)  47.2 us
    psum x1, blocking collectives, body(): lax.psum((grad_gain_one, grad_gain_two, grad_router_w), everywhere)  39.9 us
    dot_general x17, matrix products, dot(): return jnp.dot(a, b, preferred_element_type=F32)  37.3 us
    dot_general x17, matrix products, t_dot(): lax.dot_general(a, b, (((0,), (0,)), ((), ())), preferred_element_type=F32)  36.6 us
  transfers between devices with their start and end apart: 10, of which 7 were waited for; matrix products, arithmetic and copies ran while one was open for 10% of the time, Pallas kernels for 0%

profile of v1, /device:TPU:1, one launch (start us, length us, event | category | flops | bytes accessed | tf_op | source)
XLA Modules:
  0.0 1278.9 jit_solution(3100827052793407418)
XLA Ops:
  19.1 3.9 copy.122
  27.2 14.6 %all-gather.6.cloned.1.call-done = bf16[512,1024]{1,0:T(8,128)(2,1)} async-done(((bf16[256,1024]{1,0:T(8,128)(2,1)}), bf16[512,1024]{1,0:T(8,128)(2,1)}) %all-gather.6.cloned.1.call-update) | async-done | bytes 1048592 | tf_op jit(solution)/shard_map/all_gather | solution.py:103
  46.1 8.0 fusion.203
  54.1 4.3 fusion.74
  61.6 6.1 all-gather
  67.8 4.6 fusion.16
  80.3 11.1 all-gather.8.cloned.1.call-done
  102.5 3.8 multiply_convert_fusion.1
  133.9 9.2 add_convert_fusion
  156.7 4.3 fusion.47
  182.8 30.6 %reduce-scatter.4.cloned.1.call-done = bf16[256,1024]{0,1:T(8,128)(2,1)} async-done(((bf16[1024,1024]{0,1:T(8,128)(2,1)}), bf16[256,1024]{0,1:T(8,128)(2,1)}) %reduce-scatter.4.cloned.1.call-update) | async-done | bytes 524304 | tf_op jit(solution)/shard_map/reduce_scatter | solution.py:177
  218.9 4.9 fusion.1
  223.9 4.8 fusion.78
  228.7 4.5 fusion.3
  247.5 3.8 pad_maximum_fusion
  264.7 423.8 %all-reduce.13.cloned.1.call-done = (bf16[4,1024,512]{2,1,0:T(8,128)(2,1)}, bf16[4,1024,512]{2,1,0:T(8,128)(2,1)}, bf16[4,512,1024]{2,1,0:T(8,128)(2,1)}) async-done(((bf16[4,1024,512]{2,1,0:T(8,128)(2,1)}, bf16[4,1024,512]{2,1,0:T(8,128)(2,1)}, bf16[4,512,1024]{2,1,0:T(8,128)(2,1)}), (bf16[4,1024,512]{2,1,0:T(8,128)(2,1)}, bf16[4,1024,512]{2,1,0:T(8,128)(2,1)}, ...) | async-done | bytes 12582928 | tf_op jit(solution)/shard_map/psum | solution.py:181
  700.5 39.9 %all-reduce = (f32[1024]{0:T(1024)}, f32[1024]{0:T(1024)}) all-reduce(f32[1024]{0:T(1024)S(1)} %get-tuple-element.26, f32[1024]{0:T(1024)S(1)} %get-tuple-element.24), channel_id=1, replica_groups=mesh['expert'=4,'context'=2,'dp'=4] {'expert','context','dp'}, use_global_device_ids=true, to_apply=%region_21.22 | all-reduce | flops 2048 | bytes 16384 | tf_op jit(solution)/shard_map/psum | solution.py:245
  740.4 112.2 %all-reduce.11.cloned.1.call-done = (bf16[1024,1024]{1,0:T(8,128)(2,1)}, bf16[1024,512]{1,0:T(8,128)(2,1)}, bf16[1024,512]{1,0:T(8,128)(2,1)}, bf16[1024,1024]{1,0:T(8,128)(2,1)}) async-done(((bf16[1024,1024]{1,0:T(8,128)(2,1)}, bf16[1024,512]{1,0:T(8,128)(2,1)}, bf16[1024,512]{1,0:T(8,128)(2,1)}, bf16[1024,1024]{1,0:T(8,128)(2,1)}), (bf16[1024,1024]{1,0:T(8,128)(2,1)}, bf16[1024,512]{1,0:T(8,128)(2,1)}, ...) | async-done | bytes 6291472 | tf_op jit(solution)/shard_map/psum | solution.py:241
  852.6 4.2 convert_element_type.280
  863.2 281.8 %all-reduce.15.cloned.1.call-done = (bf16[4,1024,512]{2,1,0:T(8,128)(2,1)}, bf16[4,1024,512]{2,1,0:T(8,128)(2,1)}, bf16[4,512,1024]{2,1,0:T(8,128)(2,1)}) async-done(((bf16[4,1024,512]{2,1,0:T(8,128)(2,1)}, bf16[4,1024,512]{2,1,0:T(8,128)(2,1)}, bf16[4,512,1024]{2,1,0:T(8,128)(2,1)}), (bf16[4,1024,512]{2,1,0:T(8,128)(2,1)}, bf16[4,1024,512]{2,1,0:T(8,128)(2,1)}, ...) | async-done | bytes 12582928 | tf_op jit(solution)/shard_map/psum | solution.py:181
  1145.0 6.9 convert_element_type.291
  1151.9 4.6 convert_element_type.296
  1156.5 4.4 convert_element_type.301
  1160.9 109.4 %all-reduce.9.cloned.1.call-done = f32[1024,16]{0,1:T(8,128)} async-done(((f32[1024,16]{0,1:T(8,128)}), f32[1024,16]{0,1:T(8,128)}) %all-reduce.9.cloned.1.call-update) | async-done | bytes 65552 | tf_op jit(solution)/shard_map/psum | solution.py:245
  (311 shorter events, 157.7 us)
Async XLA Ops:
  7.2 51.3 %copy-start = (bf16[1024,1024]{1,0:T(8,128)(2,1)S(1)}, bf16[1024,1024]{1,0:T(8,128)(2,1)}, u32[]{:S(2)}) copy-start(bf16[1024,1024]{1,0:T(8,128)(2,1)} %param.21) | copy-start | bytes 6291460
  7.2 34.6 %all-gather.6.cloned.1.call-start = ((), (), s32[]{:S(2)}) async-start(), calls=%async_computation.3 | async-start | bytes 1572864 | tf_op jit(solution)/shard_map/all_gather | solution.py:103
  8.6 49.8 %copy-start.2 = (bf16[1,256,1024]{1,2,0:T(8,128)(2,1)}, bf16[1,256,1024]{1,2,0:T(8,128)(2,1)S(1)}, u32[]{:S(2)}) copy-start(bf16[1,256,1024]{1,2,0:T(8,128)(2,1)S(1)} %copy.116) | copy-start | bytes 1572868
  9.4 13.6 %copy-start.62 = (f32[1024]{0:T(1024)}, f32[1024]{0:T(1024)S(1)}, u32[]{:S(2)}) copy-start(f32[1024]{0:T(1024)S(1)} %convert_element_type.237) | copy-start | bytes 12292
  9.5 13.5 %copy-start.64 = (f32[256]{0:T(256)}, f32[256]{0:T(256)S(1)}, u32[]{:S(2)}) copy-start(f32[256]{0:T(256)S(1)} %add_rsqrt_fusion.1) | copy-start | bytes 3076
  16.1 10.2 copy-start.47
  18.2 49.6 %all-gather.10.cloned.1.call-start = ((), (), s32[]{:S(2)}) async-start(), calls=%async_computation.9 | async-start | bytes 2621440 | tf_op jit(solution)/shard_map/all_gather | solution.py:88
  18.9 72.4 %all-gather.8.cloned.1.call-start = ((), (), s32[]{:S(2)}) async-start(), calls=%async_computation.4 | async-start | bytes 2621440 | tf_op jit(solution)/shard_map/all_gather | solution.py:128
  27.2 18.9 %copy-start.42 = (bf16[256,16,32]{0,2,1:T(8,128)(2,1)}, bf16[256,16,32]{0,2,1:T(8,128)(2,1)S(1)}, u32[]{:S(2)}) copy-start(bf16[256,16,32]{0,2,1:T(8,128)(2,1)S(1)} %get-tuple-element.60) | copy-start | bytes 786436
  27.2 18.9 %copy-start.61 = (pred[256,512]{0,1:T(8,128)(4,1)S(1)}, pred[256,512]{0,1:T(8,128)(4,1)}, u32[]{:S(2)}) copy-start(pred[256,512]{0,1:T(8,128)(4,1)} %broadcast_compare_fusion) | copy-start | bytes 393220
  61.5 117.7 %reduce-scatter.6.cloned.1.call-start = ((), (), s32[]{:S(2)}) async-start(), calls=%async_computation.6 | async-start | bytes 2949120 | tf_op jit(solution)/shard_map/reduce_scatter | solution.py:176
  77.7 13.7 %copy-start.59 = (bf16[1024,16]{0,1:T(8,128)(2,1)S(1)}, bf16[1024,16]{0,1:T(8,128)(2,1)}, u32[]{:S(2)}) copy-start(bf16[1024,16]{0,1:T(8,128)(2,1)} %param.23) | copy-start | bytes 98308
  106.3 10.4 copy-start.76
  109.0 10.3 copy-start.74
  109.0 37.1 %copy-start.21 = (bf16[1024,512]{0,1:T(8,128)(2,1)}, bf16[1024,512]{0,1:T(8,128)(2,1)S(1)}, u32[]{:S(2)}) copy-start(bf16[1024,512]{0,1:T(8,128)(2,1)S(1)} %get-tuple-element.57) | copy-start | bytes 3145732
  112.5 11.4 copy-start.77
  116.0 11.2 copy-start.85
  116.0 14.7 %copy-start.81 = (bf16[1024,512]{0,1:T(8,128)(2,1)}, bf16[1024,512]{0,1:T(8,128)(2,1)S(1)}, u32[]{:S(2)}) copy-start(bf16[1024,512]{0,1:T(8,128)(2,1)S(1)} %get-tuple-element.52) | copy-start | bytes 3145732
  146.0 67.4 %reduce-scatter.4.cloned.1.call-start = ((), (), s32[]{:S(2)}) async-start(), calls=%async_computation.5 | async-start | bytes 2621440 | tf_op jit(solution)/shard_map/reduce_scatter | solution.py:177
  154.6 105.9 %reduce-scatter.8.cloned.1.call-start = ((), (), s32[]{:S(2)}) async-start(), calls=%async_computation.7 | async-start | bytes 1572864 | tf_op jit(solution)/shard_map/reduce_scatter | solution.py:207
  236.3 452.2 %all-reduce.13.cloned.1.call-start = ((), (), s32[]{:S(2)}) async-start(), calls=%async_computation.11 | async-start | bytes 25165824 | tf_op jit(solution)/shard_map/psum | solution.py:181
  251.3 601.3 %all-reduce.11.cloned.1.call-start = ((), (), s32[]{:S(2)}) async-start(), calls=%async_computation.10 | async-start | bytes 12582912 | tf_op jit(solution)/shard_map/psum | solution.py:241
  264.7 880.3 %all-reduce.15.cloned.1.call-start = ((), (), s32[]{:S(2)}) async-start(), calls=%async_computation.12 | async-start | bytes 25165824 | tf_op jit(solution)/shard_map/psum | solution.py:181
  688.5 581.8 %all-reduce.9.cloned.1.call-start = ((), (), s32[]{:S(2)}) async-start(), calls=%async_computation.8 | async-start | bytes 131072 | tf_op jit(solution)/shard_map/psum | solution.py:245
  (77 other events, 227.6 us)
Sparse Core Ops, SparseCore 0:
  18.3 23.4 all-gather.5
  43.3 22.9 all-gather.9
  68.5 22.8 all-gather.7
  146.1 32.6 reduce-scatter.5
  181.9 31.4 reduce-scatter.3
  236.4 20.3 reduce-scatter.7
  261.0 427.4 all-reduce.12
  696.1 156.4 all-reduce.10
  855.3 289.6 all-reduce.14
  1151.0 119.2 all-reduce.8
